TPU v7x, 32 devices: a whole 2x2x4 slice. The times are simulated.
32 devices in a mesh: sub: 8 (over z, x), grp: 4 (over y, core).
Axes of the slice: x: 2, y: 2, z: 4, core: 2. Of those that a mesh axis runs over, the one named last changes fastest.
Arguments:
- loads: float32 [4, 16, 2, 48, 256], P('grp', 'sub'), may hold values from -18 to 18
- inv_schur: bfloat16 [4, 16, 1024, 1024], P('grp', 'sub'), as said below
- schur: bfloat16 [4, 16, 1024, 1024], P('grp', 'sub'), as said below
- coarse_map: bfloat16 [4, 16, 12, 1024], P('grp', 'sub'), may hold values from -0.75 to 0.75
- coarse_inverse: float32 [4, 16, 12, 4, 192], P('grp', 'sub'), as said below
- face_rows: int32 [4, 16, 1024], P('grp', 'sub'), may hold values from 0 to 1023, each once within a row
- face_len: int32 [4, 16, 2], P('grp', 'sub'), may hold values from 64 to 256
Outputs:
- multipliers: float32 [4, 16, 2, 48, 256], P('grp', 'sub')
- residual: float32 [4, 16, 2, 48, 256], P('grp', 'sub')
Inputs may be any that keep to these rules, and one draw needn't show every extreme that they name: `inv_schur`: each subdomain's matrix is symmetric and positive definite. `schur`: each subdomain's matrix is symmetric and positive definite. `coarse_inverse`: seen as a [768, 768] matrix it is symmetric and positive definite. `face_rows`: each subdomain's row is a permutation of 0 to 1023.
All inputs are finite; a program needn't handle non-finite values.
Results may differ from a plain program's by a relative error of at most 0.025.
Values sent between devices are 32-bit elements; how exact they have to be, the bound alone decides.
A program may use at most 128 MiB of HBM per device.

v0:
```python
import jax
import jax.numpy as jnp
from jax import lax
from jax.sharding import PartitionSpec as P

FACE = 256
LOADS = 48
CDOF = 12
ITERS = 3


def shifted(value, axis, steps):
    count = lax.axis_size(axis)
    initial, last = (max(0, -steps), min(count, count - steps))
    return lax.ppermute(value, axis, [(source, source + steps) for source in range(initial, last)])


def passed_along(block, axis, distance):
    devices = range(lax.axis_size(axis))
    route = [((i - distance) % len(devices), i) for i in devices]
    return lax.ppermute(block, axis, route)


def pair_sum(first, second, pattern):
    return jnp.einsum(pattern, first, second, precision=lax.Precision.HIGHEST)


def combine(weights, faces):
    return jnp.einsum("ab,gksat->gksbt", weights, faces, precision=lax.Precision.HIGHEST)


def gram_solve(matrix, right):
    return jax.scipy.linalg.cho_solve((jnp.linalg.cholesky(matrix), True), right)


def to_slots(faces):
    along = faces[0, :, 0]
    beside_all = faces[0, :, 1]
    from_left = shifted(along[1:2], "sub", 1)
    from_left = jnp.concatenate([from_left, along[0:1]], axis=0)
    from_below = passed_along(beside_all, "grp", 1)
    stacked = jnp.stack([-from_left, along, -from_below, beside_all], axis=2)
    return stacked.reshape(stacked.shape[0], stacked.shape[1], -1)


def to_faces(field, live_mask):
    pieces = field.reshape(field.shape[0], field.shape[1], 4, -1)
    from_right = shifted(pieces[0:1, :, 0], "sub", -1)
    neighbour = jnp.concatenate([pieces[1:2, :, 0], from_right], axis=0)
    from_above = passed_along(pieces[:, :, 2], "grp", -1)
    jumps = jnp.stack([pieces[:, :, 1] - neighbour, pieces[:, :, 3] - from_above], axis=1)
    return jumps[None] * live_mask


def body(loads, inv_schur, schur, coarse_map, coarse_inverse, face_rows, face_len):
    slot_rows = face_rows[0]
    permute = jax.vmap(lambda matrix, ordering: matrix[ordering][:, ordering])
    solve_mats = permute(inv_schur[0], slot_rows)
    dirichlet = permute(schur[0], slot_rows)
    coarse_basis = jax.vmap(lambda basis_rows, ordering: basis_rows[:, ordering])(
        coarse_map[0], slot_rows
    )
    own_rows = coarse_inverse[0].reshape(2 * CDOF, coarse_inverse.shape[3], coarse_inverse.shape[4])
    positions = jnp.arange(FACE)
    column = 2 * lax.axis_index("sub") + jnp.arange(2)
    last_column = 2 * lax.axis_size("sub") - 1
    along_live = (positions[None, :] < face_len[0, :, 0:1]) & (column[:, None] < last_column)
    around_live = positions[None, :] < face_len[0, :, 1:2]
    live_mask = jnp.stack([along_live, around_live], axis=1).astype(jnp.float32)[
        None, :, :, None, :
    ]

    def precondition(resid):
        slotted = to_slots(resid)
        smoothed = jnp.einsum(
            "krm,kmn->krn",
            slotted.astype(jnp.bfloat16),
            dirichlet,
            preferred_element_type=jnp.float32,
        )
        filtered = to_faces(smoothed, live_mask)
        product = lax.psum(pair_sum(filtered, resid, "gksat,gksbt->ab"), ("sub", "grp"))
        return (filtered, product)

    residual = loads * live_mask
    multipliers = jnp.zeros_like(residual)
    search, precond_gram = precondition(residual)
    direction = search
    for iteration in range(ITERS):
        operator_slotted = to_slots(direction)
        rounded = operator_slotted.astype(jnp.bfloat16)
        local_part = jnp.einsum(
            "krm,kmn->krn", rounded, solve_mats, preferred_element_type=jnp.float32
        )
        operator_coarse_terms = jnp.einsum(
            "krm,kqm->krq", rounded, coarse_basis, preferred_element_type=jnp.float32
        )
        flat_terms = jnp.transpose(operator_coarse_terms, (1, 0, 2)).reshape(1, LOADS, 2 * CDOF)
        cycle_terms = lax.all_gather(flat_terms, "grp", axis=0, tiled=True)
        solved = jnp.einsum(
            "grx,kgx->rk",
            lax.all_gather(cycle_terms, "sub", axis=2, tiled=True),
            own_rows,
            precision=lax.Precision.HIGHEST,
        )
        corrections = jnp.transpose(solved.reshape(LOADS, 2, CDOF), (1, 0, 2)).astype(jnp.bfloat16)
        response = local_part + jnp.einsum(
            "krq,kqm->krm", corrections, coarse_basis, preferred_element_type=jnp.float32
        )
        image_faces = to_faces(response, live_mask)
        curvature = lax.psum(pair_sum(direction, image_faces, "gksat,gksbt->ab"), ("sub", "grp"))
        image_faces, curvature = (image_faces, curvature)
        step_size = gram_solve(curvature, precond_gram)
        multipliers = multipliers + combine(step_size, direction)
        residual = residual - combine(step_size, image_faces)
        if iteration + 1 < ITERS:
            search, new_gram = precondition(residual)
            conjugate = gram_solve(precond_gram, new_gram)
            direction = search + combine(conjugate, direction)
            precond_gram = new_gram
    return (multipliers, residual)


def solution(mesh):
    in_specs = (
        P("grp", "sub", None, None, None),
        P("grp", "sub", None, None),
        P("grp", "sub", None, None),
        P("grp", "sub", None, None),
        P("grp", "sub", None, None, None),
        P("grp", "sub", None),
        P("grp", "sub", None),
    )
    out_specs = (P("grp", "sub", None, None, None), P("grp", "sub", None, None, None))
    return jax.shard_map(body, mesh=mesh, in_specs=in_specs, out_specs=out_specs, check_vma=False)
```

profile of v0, /device:TPU:10, one launch (start us, length us, event | category | flops | bytes accessed | tf_op | source)
XLA Modules:
  0.0 658.3 jit_solution(1124318638356162383)
XLA Ops:
  7.0 41.9 %gather_fusion = bf16[2048,1024]{1,0:T(8,128)(2,1)} fusion(bf16[2,1024,1024]{2,1,0:T(8,128)(2,1)} %bitcast.533, s32[2048]{0:T(1024)S(1)} %bitcast.528), kind=kCustom, calls=%fused_computation | custom fusion | bytes 8404992 | tf_op jit(solution)/shard_map/vmap()/gather | solution.py:57
  48.9 6.2 copy.171
  55.2 40.3 %gather_fusion.1 = bf16[2048,1024]{1,0:T(8,128)(2,1)} fusion(bf16[2,1024,1024]{1,2,0:T(8,128)(2,1)} %copy.171, s32[2048]{0:T(1024)S(1)} %bitcast.529), kind=kCustom, calls=%fused_computation.1 | custom fusion | bytes 8404992 | tf_op jit(solution)/shard_map/vmap()/gather | solution.py:57
  95.5 42.0 %gather_fusion.2 = bf16[2048,1024]{1,0:T(8,128)(2,1)} fusion(bf16[2,1024,1024]{2,1,0:T(8,128)(2,1)} %bitcast.534, s32[2048]{0:T(1024)S(1)} %bitcast.530), kind=kCustom, calls=%fused_computation.2 | custom fusion | bytes 8404992 | tf_op jit(solution)/shard_map/vmap()/gather | solution.py:57
  137.5 6.2 copy.182
  143.8 40.4 %gather_fusion.3 = bf16[2048,1024]{1,0:T(8,128)(2,1)} fusion(bf16[2,1024,1024]{1,2,0:T(8,128)(2,1)} %copy.182, s32[2048]{0:T(1024)S(1)} %bitcast.531), kind=kCustom, calls=%fused_computation.3 | custom fusion | bytes 8404992 | tf_op jit(solution)/shard_map/vmap()/gather | solution.py:57
  184.5 11.1 %gather_fusion.4 = bf16[2048,12]{1,0:T(8,128)(2,1)S(1)} fusion(bf16[2,12,1024]{1,2,0:T(8,128)(2,1)S(1)} %bitcast.549, s32[2048]{0:T(1024)S(1)} %bitcast.532), kind=kCustom, calls=%fused_computation.4 | custom fusion | bytes 114688 | tf_op jit(solution)/shard_map/vmap()/gather | solution.py:60
  206.9 3.9 collective-permute-start.4
  216.7 5.2 all_gather.18
  221.9 26.2 %all_gather.19 = f32[4,48,192]{1,2,0:T(8,128)S(1)} all-gather(f32[4,48,24]{1,2,0:T(8,128)S(1)} %all_gather.18), channel_id=1, replica_groups=mesh['sub'=8,'grp'=4] {'sub'}, dimensions={2}, use_global_device_ids=true | all-gather | bytes 165888 | tf_op jit(solution)/shard_map/all_gather | solution.py:102
  249.1 4.3 collective-permute-start.6
  256.8 43.6 %all-reduce = (f32[48,48]{0,1:T(8,128)S(1)}, f32[48,48]{0,1:T(8,128)S(1)}) all-reduce(f32[48,48]{0,1:T(8,128)S(1)} %convolution_bitcast_fusion.14, f32[48,48]{0,1:T(8,128)S(1)} %convolution_bitcast_fusion.15), channel_id=1, replica_groups=mesh['sub'=8,'grp'=4] {'sub','grp'}, use_global_device_ids=true, to_apply=%region_3.5 | all-reduce | flops 4608 | bytes 36864 | tf_op jit(solution)/shard_map/psum | solution.py:82
  300.6 4.4 cholesky.89
  313.2 4.4 cholesky.100
  318.9 3.7 custom-call.22
  326.6 3.9 collective-permute-start.10
  334.8 40.7 %psum.44 = f32[48,48]{0,1:T(8,128)S(1)} all-reduce(f32[48,48]{0,1:T(8,128)S(1)} %convolution_bitcast_fusion.13), channel_id=1, replica_groups=mesh['sub'=8,'grp'=4] {'sub','grp'}, use_global_device_ids=true, to_apply=%region_4.0 | all-reduce | flops 2304 | bytes 18432 | tf_op jit(solution)/shard_map/psum | solution.py:82
  376.5 4.4 cholesky.122
  387.9 4.0 collective-permute-done.13
  395.8 5.4 all_gather.20
  401.2 26.6 %all_gather.21 = f32[4,48,192]{1,2,0:T(8,128)S(1)} all-gather(f32[4,48,24]{1,2,0:T(8,128)S(1)} %all_gather.20), channel_id=1, replica_groups=mesh['sub'=8,'grp'=4] {'sub'}, dimensions={2}, use_global_device_ids=true | all-gather | bytes 165888 | tf_op jit(solution)/shard_map/all_gather | solution.py:102
  428.7 5.9 collective-permute-start.14
  437.8 43.5 %psum.45 = f32[48,48]{0,1:T(8,128)S(1)} all-reduce(f32[48,48]{0,1:T(8,128)S(1)} %convolution_bitcast_fusion.12), channel_id=1, replica_groups=mesh['sub'=8,'grp'=4] {'sub','grp'}, use_global_device_ids=true, to_apply=%region_5.0 | all-reduce | flops 2304 | bytes 18432 | tf_op jit(solution)/shard_map/psum | solution.py:111
  481.4 4.4 cholesky.111
  501.5 3.9 collective-permute-start.18
  508.8 41.7 %psum.46 = f32[48,48]{1,0:T(8,128)S(1)} all-reduce(f32[48,48]{1,0:T(8,128)S(1)} %convolution_bitcast_fusion.11), channel_id=1, replica_groups=mesh['sub'=8,'grp'=4] {'sub','grp'}, use_global_device_ids=true, to_apply=%region_6.9 | all-reduce | flops 2304 | bytes 18432 | tf_op jit(solution)/shard_map/psum | solution.py:82
  553.3 4.0 collective-permute-done.20
  561.3 5.4 all_gather.22
  566.7 26.5 %all_gather.23 = f32[4,48,192]{1,2,0:T(8,128)S(1)} all-gather(f32[4,48,24]{1,2,0:T(8,128)S(1)} %all_gather.22), channel_id=1, replica_groups=mesh['sub'=8,'grp'=4] {'sub'}, dimensions={2}, use_global_device_ids=true | all-gather | bytes 165888 | tf_op jit(solution)/shard_map/all_gather | solution.py:102
  594.2 5.9 collective-permute-start.22
  603.0 43.4 %psum.47 = f32[48,48]{0,1:T(8,128)S(1)} all-reduce(f32[48,48]{0,1:T(8,128)S(1)} %convolution_bitcast_fusion.10), channel_id=1, replica_groups=mesh['sub'=8,'grp'=4] {'sub','grp'}, use_global_device_ids=true, to_apply=%region_7.10 | all-reduce | flops 2304 | bytes 18432 | tf_op jit(solution)/shard_map/psum | solution.py:111
  646.4 4.4 cholesky.133
  (225 shorter events, 98.3 us)
Async XLA Ops:
  0.6 247.5 %copy-start = (f32[1,2,12,4,192]{4,3,2,1,0:T(4,128)S(1)}, f32[1,2,12,4,192]{4,3,2,1,0:T(4,128)}, u32[]{:S(2)}) copy-start(f32[1,2,12,4,192]{4,3,2,1,0:T(4,128)} %param.14) | copy-start | bytes 221188
  2.7 193.0 %collective-permute-start = (f32[1,48,256]{2,1,0:T(8,128)S(1)}, f32[1,48,256]{2,1,0:T(8,128)S(1)}, u32[]{:S(2)}, u32[]{:S(2)}) collective-permute-start(f32[1,48,256]{2,1,0:T(8,128)S(1)} %get-tuple-element.64), channel_id=1, source_target_pairs={{0,4},{4,8},{8,12},{12,16},{16,20},{20,24},{24,28},{1,5},{5,9},{9,... | collective-permute-start | bytes 147464 | tf_op jit(solution)/shard_map/ppermute | solution.py:15
  6.2 189.5 %collective-permute-start.1 = (f32[2,48,256]{2,1,0:T(8,128)S(1)}, f32[2,48,256]{2,1,0:T(8,128)S(1)}, u32[]{:S(2)}, u32[]{:S(2)}) collective-permute-start(f32[2,48,256]{2,1,0:T(8,128)S(1)} %slice_bitcast_fusion.5), channel_id=1, source_target_pairs={{3,0},{0,1},{1,2},{2,3},{7,4},{4,5},{5,6},{6,7},{11,8},{8,9},{9,10... | collective-permute-start | bytes 294920 | tf_op jit(solution)/shard_map/ppermute | solution.py:21
  143.8 40.4 %copy-start.2 = (bf16[1,2,12,1024]{3,1,2,0:T(2,128)(2,1)S(1)}, bf16[1,2,12,1024]{3,1,2,0:T(2,128)(2,1)}, u32[]{:S(2)}) copy-start(bf16[1,2,12,1024]{3,1,2,0:T(2,128)(2,1)} %param.13) | copy-start | bytes 147460
  199.5 15.5 %copy-start.1 = (bf16[2048,1024]{1,0:T(8,128)(2,1)S(1)}, bf16[2048,1024]{1,0:T(8,128)(2,1)}, u32[]{:S(2)}) copy-start(bf16[2048,1024]{1,0:T(8,128)(2,1)} %gather_fusion.3) | copy-start | bytes 12582916
  199.6 7.1 %collective-permute-start.2 = (f32[1,48,256]{2,1,0:T(8,128)S(1)}, f32[1,48,256]{2,1,0:T(8,128)S(1)}, u32[]{:S(2)}, u32[]{:S(2)}) collective-permute-start(f32[1,48,256]{2,1,0:T(8,128)S(1)} %bitcast.587), channel_id=1, source_target_pairs={{4,0},{8,4},{12,8},{16,12},{20,16},{24,20},{28,24},{5,1},{9,5},{13... | collective-permute-start | bytes 147464 | tf_op jit(solution)/shard_map/ppermute | solution.py:15
  202.6 4.2 collective-permute-start.3
  206.9 6.2 collective-permute-start.4
  210.9 4.1 collective-permute-start.5
  249.1 6.9 %collective-permute-start.6 = (f32[1,48,256]{2,1,0:T(8,128)S(1)}, f32[1,48,256]{2,1,0:T(8,128)S(1)}, u32[]{:S(2)}, u32[]{:S(2)}) collective-permute-start(f32[1,48,256]{2,1,0:T(8,128)S(1)} %bitcast.588), channel_id=1, source_target_pairs={{4,0},{8,4},{12,8},{16,12},{20,16},{24,20},{28,24},{5,1},{9,5},{13... | collective-permute-start | bytes 147464 | tf_op jit(solution)/shard_map/ppermute | solution.py:15
  253.7 2.5 collective-permute-start.7
  311.2 11.4 %collective-permute-start.8 = (f32[1,48,256]{2,1,0:T(8,128)S(1)}, f32[1,48,256]{2,1,0:T(8,128)S(1)}, u32[]{:S(2)}, u32[]{:S(2)}) collective-permute-start(f32[1,48,256]{2,1,0:T(8,128)S(1)} %get-tuple-element.54), channel_id=1, source_target_pairs={{0,4},{4,8},{8,12},{12,16},{16,20},{20,24},{24,28},{1,5},{5,9},{9,... | collective-permute-start | bytes 147464 | tf_op jit(solution)/shard_map/ppermute | solution.py:15
  313.1 9.5 %collective-permute-start.9 = (f32[2,48,256]{2,1,0:T(8,128)S(1)}, f32[2,48,256]{2,1,0:T(8,128)S(1)}, u32[]{:S(2)}, u32[]{:S(2)}) collective-permute-start(f32[2,48,256]{2,1,0:T(8,128)S(1)} %slice_bitcast_fusion.3), channel_id=1, source_target_pairs={{3,0},{0,1},{1,2},{2,3},{7,4},{4,5},{5,6},{6,7},{11,8},{8,9},{9,10... | collective-permute-start | bytes 294920 | tf_op jit(solution)/shard_map/ppermute | solution.py:21
  326.6 6.9 %collective-permute-start.10 = (f32[1,48,256]{2,1,0:T(8,128)S(1)}, f32[1,48,256]{2,1,0:T(8,128)S(1)}, u32[]{:S(2)}, u32[]{:S(2)}) collective-permute-start(f32[1,48,256]{2,1,0:T(8,128)S(1)} %bitcast.589), channel_id=1, source_target_pairs={{4,0},{8,4},{12,8},{16,12},{20,16},{24,20},{28,24},{5,1},{9,5},{13... | collective-permute-start | bytes 147464 | tf_op jit(solution)/shard_map/ppermute | solution.py:15
  330.8 3.7 collective-permute-start.11
  381.6 6.3 collective-permute-start.12
  387.8 4.1 collective-permute-start.13
  428.7 7.7 %collective-permute-start.14 = (f32[1,48,256]{2,1,0:T(8,128)S(1)}, f32[1,48,256]{2,1,0:T(8,128)S(1)}, u32[]{:S(2)}, u32[]{:S(2)}) collective-permute-start(f32[1,48,256]{2,1,0:T(8,128)S(1)} %bitcast.590), channel_id=1, source_target_pairs={{4,0},{8,4},{12,8},{16,12},{20,16},{24,20},{28,24},{5,1},{9,5},{13... | collective-permute-start | bytes 147464 | tf_op jit(solution)/shard_map/ppermute | solution.py:15
  434.9 2.5 collective-permute-start.15
  491.6 6.0 collective-permute-start.16
  493.5 4.1 collective-permute-start.17
  501.5 6.9 %collective-permute-start.18 = (f32[1,48,256]{2,1,0:T(8,128)S(1)}, f32[1,48,256]{2,1,0:T(8,128)S(1)}, u32[]{:S(2)}, u32[]{:S(2)}) collective-permute-start(f32[1,48,256]{2,1,0:T(8,128)S(1)} %bitcast.591), channel_id=1, source_target_pairs={{4,0},{8,4},{12,8},{16,12},{20,16},{24,20},{28,24},{5,1},{9,5},{13... | collective-permute-start | bytes 147464 | tf_op jit(solution)/shard_map/ppermute | solution.py:15
  505.8 2.7 collective-permute-start.19
  551.3 6.0 collective-permute-start.20
  553.3 4.1 collective-permute-start.21
  594.2 7.6 %collective-permute-start.22 = (f32[1,48,256]{2,1,0:T(8,128)S(1)}, f32[1,48,256]{2,1,0:T(8,128)S(1)}, u32[]{:S(2)}, u32[]{:S(2)}) collective-permute-start(f32[1,48,256]{2,1,0:T(8,128)S(1)} %bitcast.592), channel_id=1, source_target_pairs={{4,0},{8,4},{12,8},{16,12},{20,16},{24,20},{28,24},{5,1},{9,5},{13... | collective-permute-start | bytes 147464 | tf_op jit(solution)/shard_map/ppermute | solution.py:15
  600.4 2.3 collective-permute-start.23
where the time goes:
time: 662 us; the launch traced here: 658 us
  blocking collectives  308 us (47%)
  local copies, waits for them, and re-layouts  193 us (29%)
  other arithmetic  49.2 us (7%)
  starting transfers between devices  47 us (7%)
  matrix products  30.1 us (5%)
  waiting for transfers between devices  28.4 us (4%)
    gather x6, local copies, waits for them, and re-layouts, body(): permute = jax.vmap(lambda matrix, ordering: matrix[ordering][:, ordering])  177 us
    psum x3, blocking collectives, precondition(): lax.psum(pair_sum(filtered, resid, 'gksat,gksbt->ab'), ('sub', 'grp'))  126 us
    psum x2, blocking collectives, body(): lax.psum(pair_sum(direction, image_faces, 'gksat,gksbt->ab'), ('sub', 'gr...  86.9 us
    all_gather x3, blocking collectives, body(): lax.all_gather(cycle_terms, 'sub', axis=2, tiled=True)  79.3 us
    ppermute x12, starting transfers between devices, shifted(): lax.ppermute(value, axis, [(source, source + steps) for source in range(i...  41.7 us
    another operation x15, other arithmetic, gram_solve(): jnp.linalg.cholesky(matrix)  25.3 us
    another operation x10, other arithmetic, gram_solve(): jax.scipy.linalg.cho_solve((jnp.linalg.cholesky(matrix), True), right)  21.6 us
    ppermute x12, waiting for transfers between devices, shifted(): lax.ppermute(value, axis, [(source, source + steps) for source in range(i...  19.5 us
  transfers between devices with their start and end apart: 24, of which 15 were waited for; matrix products, arithmetic and copies ran while one was open for 31% of the time, Pallas kernels for 0%

commit v1 on v0

--- a/solution.py
+++ b/solution.py
@@ -79,7 +79,7 @@
             preferred_element_type=jnp.float32,
         )
         filtered = to_faces(smoothed, live_mask)
-        product = lax.psum(pair_sum(filtered, resid, "gksat,gksbt->ab"), ("sub", "grp"))
+        product = lax.psum(lax.psum(pair_sum(filtered, resid, "gksat,gksbt->ab"), "grp"), "sub")
         return (filtered, product)
 
     residual = loads * live_mask

time: 662 us -> 719 us (1.086); the launches traced: 658 us -> 707 us
  blocking collectives: 308 us -> 348 us
  starting transfers between devices: 47 us -> 55.3 us
    psum x2 -> x3, blocking collectives: 86.9 us -> 130 us  [body(): lax.psum(pair_sum(direction, image_faces, 'gksat,gksbt->ab'), ('sub', 'gr...]
    ppermute x12, starting transfers between devices: 41.7 us -> 49.9 us  [shifted(): lax.ppermute(value, axis, [(source, source + steps) for source in range(i...]
    psum x3 -> x6, blocking collectives: 126 us -> 120 us  [the longest x3 85.4 us: precondition(): lax.psum(lax.psum(pair_sum(filtered, resid, 'gksat,gksbt->ab'), 'grp'), '...]
  transfers between devices with their start and end apart: 24 -> 24, of which waited for: 15 -> 16; matrix products, arithmetic and copies ran while one was open for 31% -> 29% of each run, Pallas kernels for 0% -> 0%
where the time goes in v1:
time: 719 us; the launch traced here: 707 us
  blocking collectives  348 us (48%)
  local copies, waits for them, and re-layouts  194 us (27%)
  starting transfers between devices  55.3 us (8%)
  other arithmetic  49.2 us (7%)
  matrix products  30 us (4%)
  waiting for transfers between devices  28.3 us (4%)
    gather x6, local copies, waits for them, and re-layouts, body(): permute = jax.vmap(lambda matrix, ordering: matrix[ordering][:, ordering])  178 us
    psum x3, blocking collectives, body(): lax.psum(pair_sum(direction, image_faces, 'gksat,gksbt->ab'), ('sub', 'gr...  130 us
    psum x3, blocking collectives, precondition(): lax.psum(lax.psum(pair_sum(filtered, resid, 'gksat,gksbt->ab'), 'grp'), '...  85.4 us
    all_gather x3, blocking collectives, body(): lax.all_gather(cycle_terms, 'sub', axis=2, tiled=True)  82.9 us
    ppermute x12, starting transfers between devices, shifted(): lax.ppermute(value, axis, [(source, source + steps) for source in range(i...  49.9 us
    psum x3, blocking collectives, precondition(): lax.psum(pair_sum(filtered, resid, 'gksat,gksbt->ab'), 'grp')  34.2 us
    another operation x15, other arithmetic, gram_solve(): jnp.linalg.cholesky(matrix)  25.3 us
    another operation x10, other arithmetic, gram_solve(): jax.scipy.linalg.cho_solve((jnp.linalg.cholesky(matrix), True), right)  21.6 us
  transfers between devices with their start and end apart: 24, of which 16 were waited for; matrix products, arithmetic and copies ran while one was open for 29% of the time, Pallas kernels for 0%

profile of v1, /device:TPU:10, one launch (start us, length us, event | category | flops | bytes accessed | tf_op | source)
XLA Modules:
  0.0 707.0 jit_solution(15455465491789298326)
XLA Ops:
  7.0 42.1 %gather_fusion = bf16[2048,1024]{1,0:T(8,128)(2,1)} fusion(bf16[2,1024,1024]{2,1,0:T(8,128)(2,1)} %bitcast.533, s32[2048]{0:T(1024)S(1)} %bitcast.528), kind=kCustom, calls=%fused_computation | custom fusion | bytes 8404992 | tf_op jit(solution)/shard_map/vmap()/gather | solution.py:57
  49.1 6.2 copy.171
  55.3 40.5 %gather_fusion.1 = bf16[2048,1024]{1,0:T(8,128)(2,1)} fusion(bf16[2,1024,1024]{1,2,0:T(8,128)(2,1)} %copy.171, s32[2048]{0:T(1024)S(1)} %bitcast.529), kind=kCustom, calls=%fused_computation.1 | custom fusion | bytes 8404992 | tf_op jit(solution)/shard_map/vmap()/gather | solution.py:57
  95.9 42.1 %gather_fusion.2 = bf16[2048,1024]{1,0:T(8,128)(2,1)} fusion(bf16[2,1024,1024]{2,1,0:T(8,128)(2,1)} %bitcast.534, s32[2048]{0:T(1024)S(1)} %bitcast.530), kind=kCustom, calls=%fused_computation.2 | custom fusion | bytes 8404992 | tf_op jit(solution)/shard_map/vmap()/gather | solution.py:57
  138.0 6.2 copy.182
  144.2 40.6 %gather_fusion.3 = bf16[2048,1024]{1,0:T(8,128)(2,1)} fusion(bf16[2,1024,1024]{1,2,0:T(8,128)(2,1)} %copy.182, s32[2048]{0:T(1024)S(1)} %bitcast.531), kind=kCustom, calls=%fused_computation.3 | custom fusion | bytes 8404992 | tf_op jit(solution)/shard_map/vmap()/gather | solution.py:57
  185.1 11.1 %gather_fusion.4 = bf16[2048,12]{1,0:T(8,128)(2,1)S(1)} fusion(bf16[2,12,1024]{1,2,0:T(8,128)(2,1)S(1)} %bitcast.549, s32[2048]{0:T(1024)S(1)} %bitcast.532), kind=kCustom, calls=%fused_computation.4 | custom fusion | bytes 114688 | tf_op jit(solution)/shard_map/vmap()/gather | solution.py:60
  217.2 5.2 all_gather.18
  222.5 26.2 %all_gather.19 = f32[4,48,192]{1,2,0:T(8,128)S(1)} all-gather(f32[4,48,24]{1,2,0:T(8,128)S(1)} %all_gather.18), channel_id=1, replica_groups=mesh['sub'=8,'grp'=4] {'sub'}, dimensions={2}, use_global_device_ids=true | all-gather | bytes 165888 | tf_op jit(solution)/shard_map/all_gather | solution.py:102
  257.5 43.5 %psum.63 = f32[48,48]{0,1:T(8,128)S(1)} all-reduce(f32[48,48]{0,1:T(8,128)S(1)} %convolution_bitcast_fusion.15), channel_id=1, replica_groups=mesh['sub'=8,'grp'=4] {'sub','grp'}, use_global_device_ids=true, to_apply=%region_0.0 | all-reduce | flops 2304 | bytes 18432 | tf_op jit(solution)/shard_map/psum | solution.py:111
  301.1 4.4 cholesky.89
  310.5 10.3 %psum.64 = f32[48,48]{0,1:T(8,128)S(1)} all-reduce(f32[48,48]{0,1:T(8,128)S(1)} %convolution_bitcast_fusion.14), channel_id=1, replica_groups=mesh['sub'=8,'grp'=4] {'grp'}, use_global_device_ids=true, to_apply=%region_3.5 | all-reduce | flops 2304 | bytes 18432 | tf_op jit(solution)/shard_map/psum | solution.py:82
  320.8 27.9 %psum.65 = f32[48,48]{0,1:T(8,128)S(1)} all-reduce(f32[48,48]{0,1:T(8,128)S(1)} %psum.64), channel_id=1, replica_groups=mesh['sub'=8,'grp'=4] {'sub'}, use_global_device_ids=true, to_apply=%region_4.6 | all-reduce | flops 2304 | bytes 18432 | tf_op jit(solution)/shard_map/psum | solution.py:82
  349.9 4.7 collective-permute-start.8
  354.7 4.4 cholesky.100
  376.1 11.9 %psum.66 = f32[48,48]{0,1:T(8,128)S(1)} all-reduce(f32[48,48]{0,1:T(8,128)S(1)} %convolution_bitcast_fusion.13), channel_id=1, replica_groups=mesh['sub'=8,'grp'=4] {'grp'}, use_global_device_ids=true, to_apply=%region_5.0 | all-reduce | flops 2304 | bytes 18432 | tf_op jit(solution)/shard_map/psum | solution.py:82
  388.0 30.1 %psum.67 = f32[48,48]{0,1:T(8,128)S(1)} all-reduce(f32[48,48]{0,1:T(8,128)S(1)} %psum.66), channel_id=1, replica_groups=mesh['sub'=8,'grp'=4] {'sub'}, use_global_device_ids=true, to_apply=%region_6.0 | all-reduce | flops 2304 | bytes 18432 | tf_op jit(solution)/shard_map/psum | solution.py:82
  419.1 4.4 cholesky.122
  424.1 4.6 collective-permute-start.12
  441.1 5.2 all_gather.20
  446.3 28.4 %all_gather.21 = f32[4,48,192]{1,2,0:T(8,128)S(1)} all-gather(f32[4,48,24]{1,2,0:T(8,128)S(1)} %all_gather.20), channel_id=1, replica_groups=mesh['sub'=8,'grp'=4] {'sub'}, dimensions={2}, use_global_device_ids=true | all-gather | bytes 165888 | tf_op jit(solution)/shard_map/all_gather | solution.py:102
  475.7 6.0 collective-permute-start.14
  484.6 43.0 %psum.68 = f32[48,48]{0,1:T(8,128)S(1)} all-reduce(f32[48,48]{0,1:T(8,128)S(1)} %convolution_bitcast_fusion.12), channel_id=1, replica_groups=mesh['sub'=8,'grp'=4] {'sub','grp'}, use_global_device_ids=true, to_apply=%region_7.0 | all-reduce | flops 2304 | bytes 18432 | tf_op jit(solution)/shard_map/psum | solution.py:111
  527.7 4.4 cholesky.111
  555.1 12.0 %psum.69 = f32[48,48]{1,0:T(8,128)S(1)} all-reduce(f32[48,48]{1,0:T(8,128)S(1)} %convolution_bitcast_fusion.11), channel_id=1, replica_groups=mesh['sub'=8,'grp'=4] {'grp'}, use_global_device_ids=true, to_apply=%region_8.0 | all-reduce | flops 2304 | bytes 18432 | tf_op jit(solution)/shard_map/psum | solution.py:82
  567.1 27.4 %psum.70 = f32[48,48]{1,0:T(8,128)S(1)} all-reduce(f32[48,48]{1,0:T(8,128)S(1)} %psum.69), channel_id=1, replica_groups=mesh['sub'=8,'grp'=4] {'sub'}, use_global_device_ids=true, to_apply=%region_9.12 | all-reduce | flops 2304 | bytes 18432 | tf_op jit(solution)/shard_map/psum | solution.py:82
  595.3 4.7 collective-permute-start.20
  608.1 5.2 all_gather.22
  613.3 28.3 %all_gather.23 = f32[4,48,192]{1,2,0:T(8,128)S(1)} all-gather(f32[4,48,24]{1,2,0:T(8,128)S(1)} %all_gather.22), channel_id=1, replica_groups=mesh['sub'=8,'grp'=4] {'sub'}, dimensions={2}, use_global_device_ids=true | all-gather | bytes 165888 | tf_op jit(solution)/shard_map/all_gather | solution.py:102
  642.6 6.1 collective-permute-start.22
  651.6 43.2 %psum.71 = f32[48,48]{0,1:T(8,128)S(1)} all-reduce(f32[48,48]{0,1:T(8,128)S(1)} %convolution_bitcast_fusion.10), channel_id=1, replica_groups=mesh['sub'=8,'grp'=4] {'sub','grp'}, use_global_device_ids=true, to_apply=%region_10.13 | all-reduce | flops 2304 | bytes 18432 | tf_op jit(solution)/shard_map/psum | solution.py:111
  694.9 4.4 cholesky.133
  (229 shorter events, 119.9 us)
Async XLA Ops:
  0.6 248.0 %copy-start = (f32[1,2,12,4,192]{4,3,2,1,0:T(4,128)S(1)}, f32[1,2,12,4,192]{4,3,2,1,0:T(4,128)}, u32[]{:S(2)}) copy-start(f32[1,2,12,4,192]{4,3,2,1,0:T(4,128)} %param.14) | copy-start | bytes 221188
  2.7 193.5 %collective-permute-start = (f32[1,48,256]{2,1,0:T(8,128)S(1)}, f32[1,48,256]{2,1,0:T(8,128)S(1)}, u32[]{:S(2)}, u32[]{:S(2)}) collective-permute-start(f32[1,48,256]{2,1,0:T(8,128)S(1)} %get-tuple-element.62), channel_id=1, source_target_pairs={{0,4},{4,8},{8,12},{12,16},{16,20},{20,24},{24,28},{1,5},{5,9},{9,... | collective-permute-start | bytes 147464 | tf_op jit(solution)/shard_map/ppermute | solution.py:15
  6.2 190.1 %collective-permute-start.1 = (f32[2,48,256]{2,1,0:T(8,128)S(1)}, f32[2,48,256]{2,1,0:T(8,128)S(1)}, u32[]{:S(2)}, u32[]{:S(2)}) collective-permute-start(f32[2,48,256]{2,1,0:T(8,128)S(1)} %slice_bitcast_fusion.5), channel_id=1, source_target_pairs={{3,0},{0,1},{1,2},{2,3},{7,4},{4,5},{5,6},{6,7},{11,8},{8,9},{9,10... | collective-permute-start | bytes 294920 | tf_op jit(solution)/shard_map/ppermute | solution.py:21
  144.2 40.6 %copy-start.2 = (bf16[1,2,12,1024]{3,1,2,0:T(2,128)(2,1)S(1)}, bf16[1,2,12,1024]{3,1,2,0:T(2,128)(2,1)}, u32[]{:S(2)}) copy-start(bf16[1,2,12,1024]{3,1,2,0:T(2,128)(2,1)} %param.13) | copy-start | bytes 147460
  200.1 15.5 %copy-start.1 = (bf16[2048,1024]{1,0:T(8,128)(2,1)S(1)}, bf16[2048,1024]{1,0:T(8,128)(2,1)}, u32[]{:S(2)}) copy-start(bf16[2048,1024]{1,0:T(8,128)(2,1)} %gather_fusion.3) | copy-start | bytes 12582916
  200.2 7.1 %collective-permute-start.2 = (f32[1,48,256]{2,1,0:T(8,128)S(1)}, f32[1,48,256]{2,1,0:T(8,128)S(1)}, u32[]{:S(2)}, u32[]{:S(2)}) collective-permute-start(f32[1,48,256]{2,1,0:T(8,128)S(1)} %bitcast.587), channel_id=1, source_target_pairs={{4,0},{8,4},{12,8},{16,12},{20,16},{24,20},{28,24},{5,1},{9,5},{13... | collective-permute-start | bytes 147464 | tf_op jit(solution)/shard_map/ppermute | solution.py:15
  203.1 4.2 collective-permute-start.3
  207.4 6.3 collective-permute-start.4
  211.4 4.1 collective-permute-start.5
  249.7 6.9 collective-permute-start.6
  254.1 2.7 collective-permute-start.7
  349.9 14.2 %collective-permute-start.8 = (f32[1,48,256]{2,1,0:T(8,128)S(1)}, f32[1,48,256]{2,1,0:T(8,128)S(1)}, u32[]{:S(2)}, u32[]{:S(2)}) collective-permute-start(f32[1,48,256]{2,1,0:T(8,128)S(1)} %get-tuple-element.52), channel_id=1, source_target_pairs={{0,4},{4,8},{8,12},{12,16},{16,20},{20,24},{24,28},{1,5},{5,9},{9,... | collective-permute-start | bytes 147464 | tf_op jit(solution)/shard_map/ppermute | solution.py:15
  354.6 9.5 %collective-permute-start.9 = (f32[2,48,256]{2,1,0:T(8,128)S(1)}, f32[2,48,256]{2,1,0:T(8,128)S(1)}, u32[]{:S(2)}, u32[]{:S(2)}) collective-permute-start(f32[2,48,256]{2,1,0:T(8,128)S(1)} %slice_bitcast_fusion.3), channel_id=1, source_target_pairs={{3,0},{0,1},{1,2},{2,3},{7,4},{4,5},{5,6},{6,7},{11,8},{8,9},{9,10... | collective-permute-start | bytes 294920 | tf_op jit(solution)/shard_map/ppermute | solution.py:21
  368.0 7.1 %collective-permute-start.10 = (f32[1,48,256]{2,1,0:T(8,128)S(1)}, f32[1,48,256]{2,1,0:T(8,128)S(1)}, u32[]{:S(2)}, u32[]{:S(2)}) collective-permute-start(f32[1,48,256]{2,1,0:T(8,128)S(1)} %bitcast.589), channel_id=1, source_target_pairs={{4,0},{8,4},{12,8},{16,12},{20,16},{24,20},{28,24},{5,1},{9,5},{13... | collective-permute-start | bytes 147464 | tf_op jit(solution)/shard_map/ppermute | solution.py:15
  372.0 3.7 collective-permute-start.11
  424.1 9.0 %collective-permute-start.12 = (f32[1,48,256]{2,1,0:T(8,128)S(1)}, f32[1,48,256]{2,1,0:T(8,128)S(1)}, u32[]{:S(2)}, u32[]{:S(2)}) collective-permute-start(f32[1,48,256]{2,1,0:T(8,128)S(1)} %get-tuple-element.46), channel_id=1, source_target_pairs={{0,4},{4,8},{8,12},{12,16},{16,20},{20,24},{24,28},{1,5},{5,9},{9,... | collective-permute-start | bytes 147464 | tf_op jit(solution)/shard_map/ppermute | solution.py:15
  433.1 4.1 collective-permute-start.13
  475.7 7.7 %collective-permute-start.14 = (f32[1,48,256]{2,1,0:T(8,128)S(1)}, f32[1,48,256]{2,1,0:T(8,128)S(1)}, u32[]{:S(2)}, u32[]{:S(2)}) collective-permute-start(f32[1,48,256]{2,1,0:T(8,128)S(1)} %bitcast.590), channel_id=1, source_target_pairs={{4,0},{8,4},{12,8},{16,12},{20,16},{24,20},{28,24},{5,1},{9,5},{13... | collective-permute-start | bytes 147464 | tf_op jit(solution)/shard_map/ppermute | solution.py:15
  482.0 2.3 collective-permute-start.15
  537.9 6.0 collective-permute-start.16
  539.9 4.1 collective-permute-start.17
  547.9 6.9 collective-permute-start.18
  552.1 2.7 collective-permute-start.19
  595.3 8.6 %collective-permute-start.20 = (f32[1,48,256]{2,1,0:T(8,128)S(1)}, f32[1,48,256]{2,1,0:T(8,128)S(1)}, u32[]{:S(2)}, u32[]{:S(2)}) collective-permute-start(f32[1,48,256]{2,1,0:T(8,128)S(1)} %get-tuple-element.36), channel_id=1, source_target_pairs={{0,4},{4,8},{8,12},{12,16},{16,20},{20,24},{24,28},{1,5},{5,9},{9,... | collective-permute-start | bytes 147464 | tf_op jit(solution)/shard_map/ppermute | solution.py:15
  600.1 4.1 collective-permute-start.21
  642.6 7.9 %collective-permute-start.22 = (f32[1,48,256]{2,1,0:T(8,128)S(1)}, f32[1,48,256]{2,1,0:T(8,128)S(1)}, u32[]{:S(2)}, u32[]{:S(2)}) collective-permute-start(f32[1,48,256]{2,1,0:T(8,128)S(1)} %bitcast.592), channel_id=1, source_target_pairs={{4,0},{8,4},{12,8},{16,12},{20,16},{24,20},{28,24},{5,1},{9,5},{13... | collective-permute-start | bytes 147464 | tf_op jit(solution)/shard_map/ppermute | solution.py:15
  649.0 2.3 collective-permute-start.23
